TPU v7x, 32 devices: a whole 2x2x4 slice. The times are simulated.
32 devices in a mesh: groups: 2 (over y), tensor: 8 (over z, x), dp: 2 (over core).
Axes of the slice: x: 2, y: 2, z: 4, core: 2. Of those that a mesh axis runs over, the one named last changes fastest.
Arguments:
- x_act: bfloat16 [3072, 8192], P(('groups', 'dp'), 'tensor'), parts along dimension 0, may hold values from -6 to 6
- gate_pre: bfloat16 [3072, 28672], P(('groups', 'dp'), 'tensor'), parts along dimension 0, may hold values from -6 to 6
- up_pre: bfloat16 [3072, 28672], P(('groups', 'dp'), 'tensor'), parts along dimension 0, may hold values from -6 to 6
- out_grad: bfloat16 [3072, 8192], P(('groups', 'dp'), 'tensor'), parts along dimension 0, may hold values from -6 to 6
- down_weight: bfloat16 [28672, 8192], P('tensor'), may hold values from -0.0625 to 0.0625
- proj_input: bfloat16 [8192, 64], P('tensor'), may hold values from -0.0625 to 0.0625
- proj_gate: bfloat16 [28672, 64], P('tensor'), may hold values from -0.03125 to 0.03125
- proj_up: bfloat16 [28672, 64], P('tensor'), may hold values from -0.03125 to 0.03125
- proj_hidden: bfloat16 [28672, 64], P('tensor'), may hold values from -0.03125 to 0.03125
- proj_output: bfloat16 [8192, 64], P('tensor'), may hold values from -0.0625 to 0.0625
- target_sketch: bfloat16 [512, 12288], P(('groups', 'tensor')), parts along dimension 0, may hold values from -6 to 6
- token_ids: int32 [16, 192], P(('groups', 'dp')), parts along dimension 0, may hold values from 0 to 128255, as said below
- source_label: int32 [16], P(('groups', 'dp')), parts along dimension 0, may hold values from 0 to 3
Outputs:
- scores: float32 [16, 256], P(('groups', 'dp'), 'tensor'), parts along dimension 0
- source_scores: float32 [8, 256], P('groups', 'tensor'), parts along dimension 0
There are 2 independent parts, one for each index of `groups`. A program takes and returns all parts, laid end to end along the dimension named above; an argument that names none is the same for every part. Nothing has to cross between parts.
Inputs may be any that keep to these rules, and one draw needn't show every extreme that they name: `token_ids`: each candidate's ids are non-zero ids followed by padding zeros; its first 96 ids are non-zero, the first candidate has no padding, and the last has exactly 96 non-zero ids.
All inputs are finite; a program needn't handle non-finite values.
Results may differ from a plain program's by a relative error of at most 0.003.
Values may be sent and summed in bfloat16 or wider, within the bound.
A program may use at most 192 MiB of HBM per device.

v0:
```python
import jax
import jax.numpy as jnp
from jax import lax
from jax.sharding import PartitionSpec as P

NSRC = 4


def dotf(left, right):
    return jnp.dot(left, right, preferred_element_type=jnp.float32)


def local(
    x_act,
    gate_pre,
    up_pre,
    out_grad,
    down_weight,
    proj_input,
    proj_gate,
    proj_up,
    proj_hidden,
    proj_output,
    target_sketch,
    token_ids,
    source_label,
):
    tok_rows = x_act.shape[0]
    cands, seq_len = token_ids.shape
    rank = proj_input.shape[1]
    highest = lax.Precision.HIGHEST
    grad_hidden = lax.dot_general(
        lax.all_gather(out_grad, "tensor", axis=1, tiled=True),
        down_weight,
        (((1,), (1,)), ((), ())),
        preferred_element_type=jnp.float32,
    )
    gval = gate_pre.astype(jnp.float32)
    uval = up_pre.astype(jnp.float32)
    sig = jax.nn.sigmoid(gval)
    hidden = (gval * sig * uval).astype(jnp.bfloat16)
    grad_gate = (grad_hidden * uval * sig * (1.0 + gval * (1.0 - sig))).astype(jnp.bfloat16)
    grad_up = (grad_hidden * gval * sig).astype(jnp.bfloat16)
    mask = (token_ids != 0).astype(jnp.float32).reshape(tok_rows)
    term_in = dotf(x_act, proj_input)
    term_gate = dotf(grad_gate, proj_gate)
    term_up = dotf(grad_up, proj_up)
    term_hid = dotf(hidden, proj_hidden)
    term_out = dotf(out_grad, proj_output)
    whole = lax.psum((term_in, term_gate, term_up, term_hid, term_out), "tensor")
    p_in = (whole[0] * mask[:, None]).reshape(cands, seq_len, rank)
    p_gate = whole[1].reshape(cands, seq_len, rank)
    p_up = whole[2].reshape(cands, seq_len, rank)
    p_hid = (whole[3] * mask[:, None]).reshape(cands, seq_len, rank)
    p_out = whole[4].reshape(cands, seq_len, rank)
    first = jnp.einsum("csi,csj->cij", p_in, p_gate, precision=highest)
    second = jnp.einsum("csi,csj->cij", p_in, p_up, precision=highest)
    third = jnp.einsum("csi,csj->cij", p_hid, p_out, precision=highest)
    sketch = jnp.concatenate(
        [
            first.reshape(cands, rank * rank),
            second.reshape(cands, rank * rank),
            third.reshape(cands, rank * rank),
        ],
        axis=1,
    )
    inv_norm = lax.rsqrt(jnp.mean(sketch * sketch, axis=1, keepdims=True) + 1e-06)
    unit = sketch * inv_norm
    scores = jnp.dot(unit, target_sketch.astype(jnp.float32).T, precision=highest) / jnp.sqrt(
        jnp.float32(3 * rank * rank)
    )
    onehot = (source_label[:, None] == jnp.arange(NSRC, dtype=jnp.int32)[None, :]).astype(
        jnp.float32
    )
    local_totals = jnp.dot(onehot.T, scores, precision=highest)
    local_counts = jnp.sum(onehot, axis=0)
    totals, counts = lax.psum((local_totals, local_counts), "dp")
    source_scores = totals / jnp.maximum(counts, 1.0)[:, None]
    return (scores, source_scores)


def solution(mesh):
    in_specs = (
        P(("groups", "dp"), "tensor"),
        P(("groups", "dp"), "tensor"),
        P(("groups", "dp"), "tensor"),
        P(("groups", "dp"), "tensor"),
        P("tensor", None),
        P("tensor", None),
        P("tensor", None),
        P("tensor", None),
        P("tensor", None),
        P("tensor", None),
        P(("groups", "tensor"), None),
        P(("groups", "dp"), None),
        P(("groups", "dp")),
    )
    out_specs = (P(("groups", "dp"), "tensor"), P("groups", "tensor"))
    return jax.shard_map(local, mesh=mesh, in_specs=in_specs, out_specs=out_specs, check_vma=False)
```

profile of v0, /device:TPU:0, one launch (start us, length us, event | category | flops | bytes accessed | tf_op | source)
XLA Modules:
  0.0 360.0 jit_solution(18141024531194097059)
XLA Ops:
  7.2 0.7 all-gather.2.cloned.1.call-update
  8.0 2.0 fusion.31
  10.0 0.2 reshape.45
  10.2 0.8 copy.25
  10.9 2.2 fusion.29
  13.1 8.3 %fusion.10 = f32[768,64]{0,1:T(8,128)} fusion(bf16[3584,64]{0,1:T(8,128)(2,1)} %param.21, bf16[768,3584]{1,0:T(8,128)(2,1)} %param.15, bf16[768,3584]{1,0:T(8,128)(2,1)} %param.14), kind=kOutput, calls=%fused_computation.16 | convolution fusion | flops 374341632 | bytes 11665408 | tf_op jit(solution)/shard_map/dot_general | solution.py:10
  21.4 167.9 %all-gather.2.cloned.1.call-done = bf16[768,8192]{1,0:T(8,128)(2,1)} async-done(((bf16[768,1024]{1,0:T(8,128)(2,1)}), bf16[768,8192]{1,0:T(8,128)(2,1)}) %all-gather.2.cloned.1.call-update) | async-done | bytes 12582928 | tf_op jit(solution)/shard_map/all_gather | solution.py:33
  189.4 54.9 %fusion.30 = f32[768,3584]{1,0:T(8,128)} fusion(bf16[768,8192]{1,0:T(8,128)(2,1)} %all-gather.2.cloned.1.call-done, bf16[3584,8192]{1,0:T(8,128)(2,1)} %param.17), kind=kOutput, calls=%fused_computation.46 | convolution fusion | flops 45097156608 | bytes 82313216 | tf_op jit(solution)/shard_map/dot_general | solution.py:32
  244.3 7.6 %fusion.12 = f32[768,64]{0,1:T(8,128)S(1)} fusion(bf16[3584,64]{0,1:T(8,128)(2,1)S(1)} %copy-done.5, f32[768,3584]{1,0:T(8,128)} %fusion.30, bf16[768,3584]{1,0:T(8,128)(2,1)} %param.14), kind=kOutput, calls=%fused_computation.17 | convolution fusion | flops 371589120 | bytes 17170432 | tf_op jit(solution)/shard_map/dot_general | solution.py:10
  251.9 1.5 copy-done.8
  253.4 7.6 %fusion.14 = f32[768,64]{0,1:T(8,128)S(1)} fusion(bf16[3584,64]{0,1:T(8,128)(2,1)S(1)} %copy-done.6, f32[768,3584]{1,0:T(8,128)S(1)} %copy-done.8, bf16[768,3584]{1,0:T(8,128)(2,1)} %param.15, bf16[768,3584]{1,0:T(8,128)(2,1)} %param.14), kind=kOutput, calls=%fused_computation.18 | convolution fusion | flops 385351680 | bytes 22675456 | tf_op jit(solution)/shard_map/dot_general | solution.py:10
  261.0 0.2 reshape.40
  261.2 0.7 copy.21
  262.1 0.7 copy.23
  263.1 79.8 %all-reduce.4.cloned.1.call-done = (f32[4,192,64]{1,2,0:T(8,128)}, f32[768,64]{0,1:T(8,128)}, f32[4,192,64]{1,2,0:T(8,128)}, f32[4,192,64]{1,2,0:T(8,128)}, f32[768,64]{0,1:T(8,128)}) async-done(((f32[4,192,64]{1,2,0:T(8,128)}, f32[768,64]{0,1:T(8,128)}, f32[4,192,64]{1,2,0:T(8,128)}, f32[4,192,64]{1,2,0:T(8,128)}, f32[768,64]{0,1:T(8,128)}), (f32[4,192,64]{1,2,0:T(8,128)}, f32[768,64]{0,1:T(8,128)}, ...) | async-done | bytes 983056 | tf_op jit(solution)/shard_map/psum | solution.py:50
  342.9 1.1 broadcast_multiply_fusion
  344.2 1.3 fusion.16
  345.8 1.3 fusion.18
  347.2 1.3 fusion.20
  348.8 0.2 multiply_reduce_fusion
  349.0 0.8 convolution_multiply_fusion
  349.8 0.3 fusion.24
  350.1 2.5 all-reduce.1
  352.5 0.7 broadcast_divide_fusion
  (34 shorter events, 1.3 us)
Async XLA Ops:
  7.2 3.8 %copy-start = (bf16[768,1024]{1,0:T(8,128)(2,1)S(1)}, bf16[768,1024]{1,0:T(8,128)(2,1)}, u32[]{:S(2)}) copy-start(bf16[768,1024]{1,0:T(8,128)(2,1)} %param.13) | copy-start | bytes 4718596
  7.2 182.2 %all-gather.2.cloned.1.call-start = ((), (), s32[]{:S(2)}) async-start(), calls=%async_computation | async-start | bytes 14155776 | tf_op jit(solution)/shard_map/all_gather | solution.py:33
  7.9 335.0 %all-reduce.4.cloned.1.call-start = ((), (), s32[]{:S(2)}) async-start(), calls=%async_computation.1 | async-start | bytes 2359296 | tf_op jit(solution)/shard_map/psum | solution.py:50
  21.4 222.9 %copy-start.5 = (bf16[3584,64]{0,1:T(8,128)(2,1)S(1)}, bf16[3584,64]{0,1:T(8,128)(2,1)}, u32[]{:S(2)}) copy-start(bf16[3584,64]{0,1:T(8,128)(2,1)} %param.20) | copy-start | bytes 1376260
  244.3 7.6 %copy-start.6 = (bf16[3584,64]{0,1:T(8,128)(2,1)S(1)}, bf16[3584,64]{0,1:T(8,128)(2,1)}, u32[]{:S(2)}) copy-start(bf16[3584,64]{0,1:T(8,128)(2,1)} %param.19) | copy-start | bytes 1376260
  244.3 9.0 %copy-start.8 = (f32[768,3584]{1,0:T(8,128)S(1)}, f32[768,3584]{1,0:T(8,128)}, u32[]{:S(2)}) copy-start(f32[768,3584]{1,0:T(8,128)} %fusion.30) | copy-start | bytes 33030148
  253.4 9.6 %copy-start.3 = (s32[4,192]{1,0:T(4,128)S(1)}, s32[4,192]{1,0:T(4,128)}, u32[]{:S(2)}) copy-start(s32[4,192]{1,0:T(4,128)} %param.24) | copy-start | bytes 9220
  253.4 9.6 %copy-start.7 = (s32[4]{0:T(128)S(1)}, s32[4]{0:T(128)}, u32[]{:S(2)}) copy-start(s32[4]{0:T(128)} %param.25) | copy-start | bytes 52
  253.4 95.7 %copy-start.2 = (bf16[32,12288]{1,0:T(8,128)(2,1)S(1)}, bf16[32,12288]{1,0:T(8,128)(2,1)}, u32[]{:S(2)}) copy-start(bf16[32,12288]{1,0:T(8,128)(2,1)} %param.23) | copy-start | bytes 2359300
  253.4 99.8 %copy-start.1 = (bf16[768,1024]{1,0:T(8,128)(2,1)S(1)}, bf16[768,1024]{1,0:T(8,128)(2,1)}, u32[]{:S(2)}) copy-start(bf16[768,1024]{1,0:T(8,128)(2,1)} %param.13) | copy-start | bytes 4718596
  349.8 3.4 copy-start.4
Sparse Core Ops, SparseCore 0:
  10.2 179.1 all-gather.1
  263.0 79.8 all-reduce.3
where the time goes:
time: 360 us
  waiting for transfers between devices  248 us (69%)
  matrix products  87.7 us (24%)
  between operations  14.2 us (4%)
  local copies, waits for them, and re-layouts  5.16 us (1%)
    all_gather x1, waiting for transfers between devices, local(): lax.all_gather(out_grad, 'tensor', axis=1, tiled=True)  168 us
    psum x1, waiting for transfers between devices, local(): lax.psum((term_in, term_gate, term_up, term_hid, term_out), 'tensor')  79.8 us
    dot_general x1, matrix products, local(): lax.dot_general(lax.all_gather(out_grad, 'tensor', axis=1, tiled=True), d...  54.9 us
    dot_general x5, matrix products, dotf(): return jnp.dot(left, right, preferred_element_type=jnp.float32)  27.7 us
  transfers between devices with their start and end apart: 2, of which 2 were waited for; matrix products, arithmetic and copies ran while one was open for 4% of the time, Pallas kernels for 0%

commit v1 on v0

--- a/solution.py
+++ b/solution.py
@@ -1,13 +1,451 @@
+import functools
+
 import jax
 import jax.numpy as jnp
 from jax import lax
+from jax.experimental import pallas as pl
+from jax.experimental.pallas import tpu as pltpu
 from jax.sharding import PartitionSpec as P
 
 NSRC = 4
+MESH = pl.DeviceIdType.MESH
+F32 = jnp.float32
+BF16 = jnp.bfloat16
+TILE = 256
 
 
 def dotf(left, right):
     return jnp.dot(left, right, preferred_element_type=jnp.float32)
+
+
+def dot_nt(left, right):
+    return lax.dot_general(left, right, (((1,), (1,)), ((), ())), preferred_element_type=F32)
+
+
+def dot_tn(left, right):
+    return lax.dot_general(
+        left, right, (((0,), (0,)), ((), ())), preferred_element_type=F32, precision=lax.Precision.HIGHEST
+    )
+
+
+def fused_kernel(
+    x_hbm, g_hbm, u_hbm, og_hbm, w_hbm, pi_hbm, pg_hbm, pu_hbm, ph_hbm, po_hbm, mask_ref,
+    out_ref,
+    gath, acc, fa, fb, wbuf, gbuf, ubuf, pi, pg, pu, ph, po, hid_acc, gate_acc, up_acc,
+    send0, send1, red0, red1, sk,
+    s_send, s_recv, s_own, s_w, s_x, s_g, s_u, s_p, s_rs, s_rr, s_ss, s_sr,
+):
+    rows, half = gath.shape[1], gath.shape[2]
+    ff = acc.shape[1]
+    tiles = ff // TILE
+    n = 8
+    part = rows // n
+    me = lax.axis_index("tensor")
+    col, z = me % 2, me // 2
+    other = 1 - col
+    flip = z // 2
+    pos = z + flip * (3 - 2 * z)
+
+    def plane(v):
+        return v + flip * (3 - 2 * v)
+
+    def tid(c, v):
+        return plane(v) * 2 + c
+
+    near, mid, far = 1 - pos, 2, 3
+    to_x, to_near, to_up = tid(other, pos), tid(col, near), tid(col, mid)
+
+    own_copies = [
+        pltpu.make_async_copy(
+            og_hbm.at[:, pl.ds(h * half, half)], gath.at[2 * me + h], s_own.at[h]
+        )
+        for h in range(2)
+    ]
+    for c in own_copies:
+        c.start()
+
+    def w_copy(slot, k):
+        return pltpu.make_async_copy(
+            w_hbm.at[:, pl.ds(pl.multiple_of(slot * half, half), half)], wbuf.at[k], s_w.at[k]
+        )
+
+    small = [
+        pltpu.make_async_copy(src, dst, s_p.at[i])
+        for i, (src, dst) in enumerate(
+            ((pi_hbm, pi), (ph_hbm, ph), (po_hbm, po), (pg_hbm, pg), (pu_hbm, pu))
+        )
+    ]
+    x_copies = [
+        pltpu.make_async_copy(
+            x_hbm.at[:, pl.ds(h * half, half)], wbuf.at[1, pl.ds(h * rows, rows)], s_x.at[h]
+        )
+        for h in range(2)
+    ]
+
+    barrier = pltpu.get_barrier_semaphore()
+    for d in range(1, n):
+        pl.semaphore_signal(
+            barrier, inc=1, device_id={"tensor": (me + d) % n}, device_id_type=MESH
+        )
+    pl.semaphore_wait(barrier, n - 1)
+
+    def piece(slot, way, target):
+        return pltpu.make_async_remote_copy(
+            src_ref=gath.at[slot], dst_ref=gath.at[slot],
+            send_sem=s_send.at[slot, way], recv_sem=s_recv.at[slot],
+            device_id={"tensor": target}, device_id_type=MESH,
+        )
+
+    def go_x(slot):
+        piece(slot, 0, to_x).start()
+
+    def go_near(slot):
+        piece(slot, 1, to_near).start()
+
+    def go_up(slot):
+        piece(slot, 2, to_up).start()
+
+    own = [2 * me, 2 * me + 1]
+    xo = [2 * to_x, 2 * to_x + 1]
+    a = [2 * tid(col, near) + h for h in range(2)]
+    b = [2 * tid(col, mid) + h for h in range(2)]
+    c = [2 * tid(col, far) + h for h in range(2)]
+    xa = [2 * tid(other, near) + h for h in range(2)]
+    xb = [2 * tid(other, mid) + h for h in range(2)]
+    xc = [2 * tid(other, far) + h for h in range(2)]
+    at1 = pos == 1
+
+    own_copies[0].wait()
+    go_x(own[0])
+    go_near(own[0])
+
+    @pl.when(at1)
+    def _():
+        go_up(own[0])
+
+    w_copy(own[0], 0).start()
+    for cp in small + x_copies:
+        cp.start()
+
+    def gu_copies(j, k):
+        cols = pl.ds(pl.multiple_of(j * TILE, TILE), TILE)
+        return (
+            pltpu.make_async_copy(g_hbm.at[:, cols], gbuf.at[k], s_g.at[k]),
+            pltpu.make_async_copy(u_hbm.at[:, cols], ubuf.at[k], s_u.at[k]),
+        )
+
+    for cp in gu_copies(0, 0):
+        cp.start()
+    hid_acc[...] = jnp.zeros_like(hid_acc)
+    gate_acc[...] = jnp.zeros_like(gate_acc)
+    up_acc[...] = jnp.zeros_like(up_acc)
+    for cp in small:
+        cp.wait()
+    chunk = rows // 6
+
+    def factors(j, carry):
+        k = j % 2
+
+        @pl.when(j + 1 < tiles)
+        def _():
+            for cp in gu_copies(j + 1, 1 - k):
+                cp.start()
+
+        for cp in gu_copies(j, k):
+            cp.wait()
+        base = pl.multiple_of(j * TILE, TILE)
+
+        def rows_of(r, carry2):
+            rs = pl.ds(pl.multiple_of(r * chunk, chunk), chunk)
+            g = gbuf[k, rs, :].astype(F32)
+            u = ubuf[k, rs, :].astype(F32)
+            s = jax.nn.sigmoid(g)
+            gs = g * s
+            fb[rs, pl.ds(base, TILE)] = gs
+            fa[rs, pl.ds(base, TILE)] = u * s * (1.0 + g * (1.0 - s))
+            hidden = (gs * u).astype(BF16)
+            hid_acc[rs, :] += dotf(hidden, ph[pl.ds(base, TILE), :])
+            return carry2
+
+        return lax.fori_loop(0, 6, rows_of, carry)
+
+    lax.fori_loop(0, tiles // 2, factors, 0)
+
+    own_copies[1].wait()
+    go_x(own[1])
+    go_near(own[1])
+
+    @pl.when(at1)
+    def _():
+        go_up(own[1])
+
+    lax.fori_loop(tiles // 2, tiles, factors, 0)
+
+    for cp in x_copies:
+        cp.wait()
+    pin = dotf(wbuf[1, 0:rows, :], pi[0:half, :]) + dotf(
+        wbuf[1, rows : 2 * rows, :], pi[half : 2 * half, :]
+    )
+    send0[:, 0:128] = jnp.concatenate(
+        [
+            pin,
+            dotf(gath[own[0]], po[0:half, :]) + dotf(gath[own[1]], po[half : 2 * half, :]),
+        ],
+        axis=1,
+    )
+    send0[:, 128:256] = jnp.concatenate([hid_acc[...], jnp.zeros((rows, 64), F32)], axis=1)
+
+    def tile_of(j):
+        return pl.ds(pl.multiple_of(j * TILE, TILE), TILE)
+
+    def matmul(slot, k, first):
+        def body(j, carry):
+            prod = dot_nt(gath[slot], wbuf[k, tile_of(j), :])
+            if first:
+                acc[:, tile_of(j)] = prod
+            else:
+                acc[:, tile_of(j)] += prod
+            return carry
+
+        lax.fori_loop(0, tiles, body, 0)
+
+    def last(slot, k):
+        def body(j, carry):
+            gh = acc[:, tile_of(j)] + dot_nt(gath[slot], wbuf[k, tile_of(j), :])
+            gg = (gh * fa[:, tile_of(j)]).astype(BF16)
+            gu = (gh * fb[:, tile_of(j)]).astype(BF16)
+            gate_acc[...] += dotf(gg, pg[tile_of(j), :])
+            up_acc[...] += dotf(gu, pu[tile_of(j), :])
+            return carry
+
+        lax.fori_loop(0, tiles, body, 0)
+
+    def reduce_copy(i, src, dst, target, source):
+        return pltpu.make_async_remote_copy(
+            src_ref=src.at[pl.ds(pl.multiple_of(target * part, part), part)],
+            dst_ref=dst.at[source],
+            send_sem=s_rs.at[i, target], recv_sem=s_rr.at[i, source],
+            device_id={"tensor": target}, device_id_type=MESH,
+        )
+
+    def nothing():
+        pass
+
+    def f_xo1():
+        @pl.when(pos == 0)
+        def _():
+            go_near(xo[1])
+
+    def f_a0():
+        go_x(a[0])
+
+        @pl.when(at1)
+        def _():
+            go_up(a[0])
+
+    def f_a1():
+        @pl.when(at1)
+        def _():
+            go_up(a[1])
+
+    def f_b0():
+        go_x(b[0])
+
+        @pl.when(at1)
+        def _():
+            go_near(b[0])
+
+    def f_b1():
+        @pl.when(at1)
+        def _():
+            go_near(b[1])
+
+        @pl.when(pos == 0)
+        def _():
+            go_x(b[1])
+
+    def f_c0():
+        go_x(c[0])
+
+        @pl.when(at1)
+        def _():
+            go_near(c[0])
+
+    def f_c1():
+        go_x(c[1])
+
+        @pl.when(at1)
+        def _():
+            go_near(c[1])
+            go_near(xo[1])
+            go_up(xo[1])
+
+    def f_last():
+        for d in range(1, n):
+            reduce_copy(0, send0, red0, (me + d) % n, me).start()
+
+    order = [
+        (own[0], None), (own[1], None),
+        (xo[0], nothing), (a[0], f_a0), (xo[1], f_xo1), (a[1], f_a1), (b[0], f_b0),
+        (xa[0], nothing), (b[1], f_b1), (c[0], f_c0), (xb[0], nothing), (c[1], f_c1),
+        (xb[1], nothing), (xc[0], nothing), (xa[1], nothing), (xc[1], f_last),
+    ]
+    steps = len(order)
+    for i, (slot, forward) in enumerate(order):
+        if i + 1 < steps:
+            w_copy(order[i + 1][0], (i + 1) % 2).start()
+        if forward is not None:
+            piece(slot, 0, to_x).wait_recv()
+            forward()
+        w_copy(slot, i % 2).wait()
+        if i + 1 < steps:
+            matmul(slot, i % 2, i == 0)
+        else:
+            last(slot, i % 2)
+
+    send1[...] = jnp.concatenate([gate_acc[...], up_acc[...]], axis=1)
+    for d in range(1, n):
+        reduce_copy(1, send1, red1, (me + d) % n, me).start()
+    mine = pl.ds(pl.multiple_of(me * part, part), part)
+    sum0, sum1 = send0[mine, :], send1[mine, :]
+    for d in range(1, n):
+        src = (me + d) % n
+        reduce_copy(0, send0, red0, src, src).wait_recv()
+        sum0 = sum0 + red0[src]
+    for d in range(1, n):
+        src = (me + d) % n
+        reduce_copy(1, send1, red1, src, src).wait_recv()
+        sum1 = sum1 + red1[src]
+    masked = sum0 * mask_ref[mine, :]
+    sk[me, 0:64, :] = dot_tn(masked[:, 0:64], sum1)
+    sk[me, 64:128, :] = dot_tn(masked[:, 128:192], sum0[:, 0:128])
+
+    def sketch_copy(target, source):
+        return pltpu.make_async_remote_copy(
+            src_ref=sk.at[source], dst_ref=sk.at[source],
+            send_sem=s_ss.at[target], recv_sem=s_sr.at[source],
+            device_id={"tensor": target}, device_id_type=MESH,
+        )
+
+    for d in range(1, n):
+        sketch_copy((me + d) % n, me).start()
+    for slot in own + [a[0], c[0], c[1], b[0]]:
+        piece(slot, 0, to_x).wait_send()
+    for slot in own:
+        piece(slot, 1, to_near).wait_send()
+
+    @pl.when(pos == 0)
+    def _():
+        piece(b[1], 0, to_x).wait_send()
+        piece(xo[1], 1, to_near).wait_send()
+
+    @pl.when(at1)
+    def _():
+        for slot in own + [a[0], a[1], xo[1]]:
+            piece(slot, 2, to_up).wait_send()
+        for slot in [b[0], b[1], c[0], c[1], xo[1]]:
+            piece(slot, 1, to_near).wait_send()
+
+    for d in range(1, n):
+        t = (me + d) % n
+        reduce_copy(0, send0, red0, t, me).wait_send()
+        reduce_copy(1, send1, red1, t, me).wait_send()
+    for d in range(1, n):
+        t = (me + d) % n
+        sketch_copy(t, t).wait_recv()
+    for d in range(1, n):
+        sketch_copy((me + d) % n, me).wait_send()
+    out_ref[...] = sk[...]
+
+
+def fused(x_act, gate_pre, up_pre, out_grad, down_weight, pi, pg, pu, ph, po, mask):
+    rows, feat = x_act.shape
+    ff = gate_pre.shape[1]
+    half = feat // 2
+    n = 8
+    rank = pi.shape[1]
+    part = rows // n
+    dma = pltpu.SemaphoreType.DMA
+    vm = pltpu.VMEM
+    any_spec = pl.BlockSpec(memory_space=pl.ANY)
+    return pl.pallas_call(
+        fused_kernel,
+        out_shape=jax.ShapeDtypeStruct((n, 2 * rank, 2 * rank), F32),
+        in_specs=[any_spec] * 10 + [pl.BlockSpec(memory_space=pltpu.VMEM)],
+        out_specs=pl.BlockSpec(memory_space=pltpu.VMEM),
+        scratch_shapes=[
+            vm((2 * n, rows, half), BF16),
+            vm((rows, ff), F32),
+            vm((rows, ff), F32),
+            vm((rows, ff), F32),
+            vm((2, ff, half), BF16),
+            vm((2, rows, TILE), BF16),
+            vm((2, rows, TILE), BF16),
+            vm((feat, rank), BF16),
+            vm((ff, rank), BF16),
+            vm((ff, rank), BF16),
+            vm((ff, rank), BF16),
+            vm((feat, rank), BF16),
+            vm((rows, rank), F32),
+            vm((rows, rank), F32),
+            vm((rows, rank), F32),
+            vm((rows, 4 * rank), F32),
+            vm((rows, 2 * rank), F32),
+            vm((n, part, 4 * rank), F32),
+            vm((n, part, 2 * rank), F32),
+            vm((n, 2 * rank, 2 * rank), F32),
+            dma((2 * n, 3)), dma((2 * n,)), dma((2,)), dma((2,)), dma((2,)), dma((2,)), dma((2,)),
+            dma((5,)), dma((2, n)), dma((2, n)), dma((n,)), dma((n,)),
+        ],
+        compiler_params=pltpu.CompilerParams(
+            collective_id=0, has_side_effects=True, vmem_limit_bytes=VLIM
+        ),
+        cost_estimate=pl.CostEstimate(
+            flops=2 * rows * ff * feat * n, bytes_accessed=2 * ff * feat * n, transcendentals=rows * ff
+        ),
+    )(x_act, gate_pre, up_pre, out_grad, down_weight, pi, pg, pu, ph, po, mask)
+
+
+VLIM = 66 * 1000 * 1000
+
+
+def tail(sketch, target_sketch, source_label):
+    highest = lax.Precision.HIGHEST
+    inv_norm = lax.rsqrt(jnp.mean(sketch * sketch, axis=1, keepdims=True) + 1e-06)
+    unit = sketch * inv_norm
+    scores = jnp.dot(unit, target_sketch.astype(F32).T, precision=highest) / jnp.sqrt(
+        F32(sketch.shape[1])
+    )
+    onehot = (source_label[:, None] == jnp.arange(NSRC, dtype=jnp.int32)[None, :]).astype(F32)
+    local_totals = jnp.dot(onehot.T, scores, precision=highest)
+    local_counts = jnp.sum(onehot, axis=0)
+    totals, counts = lax.psum((local_totals, local_counts), "dp")
+    source_scores = totals / jnp.maximum(counts, 1.0)[:, None]
+    return (scores, source_scores)
+
+
+def local_fused(
+    x_act, gate_pre, up_pre, out_grad, down_weight, proj_input, proj_gate, proj_up, proj_hidden,
+    proj_output, target_sketch, token_ids, source_label,
+):
+    rows = x_act.shape[0]
+    cands = token_ids.shape[0]
+    r = proj_input.shape[1]
+    mask = (token_ids != 0).astype(F32).reshape(rows, 1)
+    parts = fused(
+        x_act, gate_pre, up_pre, out_grad, down_weight,
+        proj_input, proj_gate, proj_up, proj_hidden, proj_output, mask,
+    )
+    mats = parts.reshape(cands, 8 // cands, 2 * r, 2 * r).sum(axis=1)
+    sketch = jnp.concatenate(
+        [
+            mats[:, :r, :r].reshape(cands, r * r),
+            mats[:, :r, r:].reshape(cands, r * r),
+            mats[:, r:, r:].reshape(cands, r * r),
+        ],
+        axis=1,
+    )
+    return tail(sketch, target_sketch, source_label)
 
 
 def local(
@@ -64,19 +502,7 @@
         ],
         axis=1,
     )
-    inv_norm = lax.rsqrt(jnp.mean(sketch * sketch, axis=1, keepdims=True) + 1e-06)
-    unit = sketch * inv_norm
-    scores = jnp.dot(unit, target_sketch.astype(jnp.float32).T, precision=highest) / jnp.sqrt(
-        jnp.float32(3 * rank * rank)
-    )
-    onehot = (source_label[:, None] == jnp.arange(NSRC, dtype=jnp.int32)[None, :]).astype(
-        jnp.float32
-    )
-    local_totals = jnp.dot(onehot.T, scores, precision=highest)
-    local_counts = jnp.sum(onehot, axis=0)
-    totals, counts = lax.psum((local_totals, local_counts), "dp")
-    source_scores = totals / jnp.maximum(counts, 1.0)[:, None]
-    return (scores, source_scores)
+    return tail(sketch, target_sketch, source_label)
 
 
 def solution(mesh):
@@ -96,4 +522,5 @@
         P(("groups", "dp")),
     )
     out_specs = (P(("groups", "dp"), "tensor"), P("groups", "tensor"))
-    return jax.shard_map(local, mesh=mesh, in_specs=in_specs, out_specs=out_specs, check_vma=False)
+    body = local_fused if mesh.shape["tensor"] == 8 else local
+    return jax.shard_map(body, mesh=mesh, in_specs=in_specs, out_specs=out_specs, check_vma=False)

time: 360 us -> 209 us (0.58)
  waiting for transfers between devices: 248 us -> 0 us
  Pallas kernels: 0 us -> 189 us
  matrix products: 87.7 us -> 1.04 us
  between operations: 14.2 us -> 0.69 us
  local copies, waits for them, and re-layouts: 5.16 us -> 11.9 us
    pallas_call x0 -> x1, Pallas kernels: none -> 189 us  [fused(): pl.pallas_call(fused_kernel, out_shape=jax.ShapeDtypeStruct((n, 2 * rank,...]
    all_gather x1 -> x0, waiting for transfers between devices: 168 us -> none  [local(): lax.all_gather(out_grad, 'tensor', axis=1, tiled=True)]
    dot_general x11 -> x2, matrix products: 87.7 us -> 1.04 us  [the longest x1 0.78 us: tail(): jnp.dot(unit, target_sketch.astype(F32).T, precision=highest)]
    psum x1 -> x0, waiting for transfers between devices: 79.8 us -> none  [local(): lax.psum((term_in, term_gate, term_up, term_hid, term_out), 'tensor')]
    unnamed x20 -> x13, local copies, waits for them, and re-layouts: 1.53 us -> 10.4 us
  transfers between devices with their start and end apart: 2 -> 0, of which waited for: 2 -> 0; matrix products, arithmetic and copies ran while one was open for 4% -> 0% of each run, Pallas kernels for 0% -> 0%
where the time goes in v1:
time: 209 us; the launch traced here: 208 us
  Pallas kernels  189 us (90%)
  local copies, waits for them, and re-layouts  11.9 us (6%)
  other arithmetic  2.77 us (1%)
  blocking collectives  2.46 us (1%)
    pallas_call x1, Pallas kernels, fused(): pl.pallas_call(fused_kernel, out_shape=jax.ShapeDtypeStruct((n, 2 * rank,...  189 us
    unnamed x13, local copies, waits for them, and re-layouts  10.4 us

profile of v1, /device:TPU:0, one launch (start us, length us, event | category | flops | bytes accessed | tf_op | source)
XLA Modules:
  0.0 208.3 jit_solution(17729890632227644365)
XLA Ops:
  0.6 0.0 copy-start
  0.6 2.3 %copy.27.pg_hbm = bf16[3584,64]{1,0:T(8,128)(2,1)} copy(bf16[3584,64]{0,1:T(8,128)(2,1)} %param.19) | data formatting | bytes 917504 | tf_op args[6]
  3.0 2.3 %copy.28.pu_hbm = bf16[3584,64]{1,0:T(8,128)(2,1)} copy(bf16[3584,64]{0,1:T(8,128)(2,1)} %param.20) | data formatting | bytes 917504 | tf_op args[7]
  5.3 2.3 %copy.29.ph_hbm = bf16[3584,64]{1,0:T(8,128)(2,1)} copy(bf16[3584,64]{0,1:T(8,128)(2,1)} %param.21) | data formatting | bytes 917504 | tf_op args[8]
  7.5 0.7 compare_convert_fusion
  8.2 1.0 reshape.39.mask_ref
  9.2 1.7 copy.26.pi_hbm
  11.0 1.8 copy.30.po_hbm
  12.7 0.0 copy-start.2
  12.7 189.4 %shard_map.140 = f32[8,128,128]{2,1,0:T(8,128)} custom-call(bf16[768,1024]{1,0:T(8,128)(2,1)} %x_hbm.1, bf16[768,3584]{1,0:T(8,128)(2,1)} %g_hbm.1, bf16[768,3584]{1,0:T(8,128)(2,1)} %u_hbm.1, bf16[768,1024]{1,0:T(8,128)(2,1)} %og_hbm.1, bf16[3584,8192]{1,0:T(8,128)(2,1)} %w_hbm.1, bf16[1024,64]{1,0:T(8,128)(2,1)} %copy.26.pi_hbm, ...), custom_call_target="tpu_custom_call" | custom-call | flops 45097156608 | bytes 58720256 | tf_op jit(solution)/shard_map/pallas_call | solution.py:371
  202.2 1.1 bitcast_reduce_fusion
  203.3 0.1 fusion.4
  203.4 0.1 reshape.34
  203.6 0.1 reshape.35
  203.7 0.1 reshape.36
  203.8 0.2 multiply_reduce_fusion
  204.0 0.0 copy-done
  204.0 0.8 convolution_multiply_fusion
  204.8 0.0 copy-done.2
  204.8 0.3 fusion.2
  205.1 0.1 convert_reduce_fusion
  205.2 2.5 %all-reduce = (f32[4,32]{1,0:T(4,128)S(1)}, f32[4]{0:T(128)S(1)}) all-reduce(f32[4,32]{1,0:T(4,128)S(1)} %fusion.2, f32[4]{0:T(128)S(1)} %convert_reduce_fusion), channel_id=1, replica_groups=mesh['groups'=2,'tensor'=8,'dp'=2] {'dp'}, use_global_device_ids=true, to_apply=%region_2.0 | all-reduce | flops 132 | bytes 1056 | tf_op jit(solution)/shard_map/psum | solution.py:422
  207.6 0.7 broadcast_divide_fusion
  208.3 0.0 copy-done.1
  (6 shorter events, 0.0 us)
Async XLA Ops:
  0.6 203.4 %copy-start = (bf16[32,12288]{1,0:T(8,128)(2,1)S(1)}, bf16[32,12288]{1,0:T(8,128)(2,1)}, u32[]{:S(2)}) copy-start(bf16[32,12288]{1,0:T(8,128)(2,1)} %param.23) | copy-start | bytes 2359300
  12.7 192.1 %copy-start.2 = (s32[4]{0:T(128)S(1)}, s32[4]{0:T(128)}, u32[]{:S(2)}) copy-start(s32[4]{0:T(128)} %param.25) | copy-start | bytes 52
  204.8 3.5 %copy-start.1 = (f32[4,32]{1,0:T(4,128)}, f32[4,32]{1,0:T(4,128)S(1)}, u32[]{:S(2)}) copy-start(f32[4,32]{1,0:T(4,128)S(1)} %convolution_multiply_fusion) | copy-start | bytes 1540

commit v2 on v1

--- a/solution.py
+++ b/solution.py
@@ -12,6 +12,8 @@
 F32 = jnp.float32
 BF16 = jnp.bfloat16
 TILE = 256
+WIDE = 1792
+TAIL = 512
 
 
 def dotf(left, right):
@@ -29,7 +31,7 @@
 
 
 def fused_kernel(
-    x_hbm, g_hbm, u_hbm, og_hbm, w_hbm, pi_hbm, pg_hbm, pu_hbm, ph_hbm, po_hbm, mask_ref,
+    x_hbm, g_hbm, u_hbm, og_hbm, w_hbm, pi_hbm, pg_hbm, pu_hbm, ph_hbm, po_hbm, ids_ref,
     out_ref,
     gath, acc, fa, fb, wbuf, gbuf, ubuf, pi, pg, pu, ph, po, hid_acc, gate_acc, up_acc,
     send0, send1, red0, red1, sk,
@@ -164,7 +166,7 @@
             fb[rs, pl.ds(base, TILE)] = gs
             fa[rs, pl.ds(base, TILE)] = u * s * (1.0 + g * (1.0 - s))
             hidden = (gs * u).astype(BF16)
-            hid_acc[rs, :] += dotf(hidden, ph[pl.ds(base, TILE), :])
+            hid_acc[rs, :] += dot_nt(hidden, ph[:, pl.ds(base, TILE)])
             return carry2
 
         return lax.fori_loop(0, 6, rows_of, carry)
@@ -183,42 +185,45 @@
 
     for cp in x_copies:
         cp.wait()
-    pin = dotf(wbuf[1, 0:rows, :], pi[0:half, :]) + dotf(
-        wbuf[1, rows : 2 * rows, :], pi[half : 2 * half, :]
+    pin = dot_nt(wbuf[1, 0:rows, :], pi[:, 0:half]) + dot_nt(
+        wbuf[1, rows : 2 * rows, :], pi[:, half : 2 * half]
     )
     send0[:, 0:128] = jnp.concatenate(
         [
             pin,
-            dotf(gath[own[0]], po[0:half, :]) + dotf(gath[own[1]], po[half : 2 * half, :]),
+            dot_nt(gath[own[0]], po[:, 0:half]) + dot_nt(gath[own[1]], po[:, half : 2 * half]),
         ],
         axis=1,
     )
     send0[:, 128:256] = jnp.concatenate([hid_acc[...], jnp.zeros((rows, 64), F32)], axis=1)
 
-    def tile_of(j):
-        return pl.ds(pl.multiple_of(j * TILE, TILE), TILE)
+    def wide(j):
+        return pl.ds(pl.multiple_of(j * WIDE, WIDE), WIDE)
+
+    def tail_of(j):
+        return pl.ds(pl.multiple_of(j * TAIL, TAIL), TAIL)
 
     def matmul(slot, k, first):
         def body(j, carry):
-            prod = dot_nt(gath[slot], wbuf[k, tile_of(j), :])
+            prod = dot_nt(gath[slot], wbuf[k, wide(j), :])
             if first:
-                acc[:, tile_of(j)] = prod
+                acc[:, wide(j)] = prod
             else:
-                acc[:, tile_of(j)] += prod
+                acc[:, wide(j)] += prod
             return carry
 
-        lax.fori_loop(0, tiles, body, 0)
+        lax.fori_loop(0, ff // WIDE, body, 0)
 
     def last(slot, k):
         def body(j, carry):
-            gh = acc[:, tile_of(j)] + dot_nt(gath[slot], wbuf[k, tile_of(j), :])
-            gg = (gh * fa[:, tile_of(j)]).astype(BF16)
-            gu = (gh * fb[:, tile_of(j)]).astype(BF16)
-            gate_acc[...] += dotf(gg, pg[tile_of(j), :])
-            up_acc[...] += dotf(gu, pu[tile_of(j), :])
+            gh = acc[:, tail_of(j)] + dot_nt(gath[slot], wbuf[k, tail_of(j), :])
+            gg = (gh * fa[:, tail_of(j)]).astype(BF16)
+            gu = (gh * fb[:, tail_of(j)]).astype(BF16)
+            gate_acc[...] += dot_nt(gg, pg[:, tail_of(j)])
+            up_acc[...] += dot_nt(gu, pu[:, tail_of(j)])
             return carry
 
-        lax.fori_loop(0, tiles, body, 0)
+        lax.fori_loop(0, ff // TAIL, body, 0)
 
     def reduce_copy(i, src, dst, target, source):
         return pltpu.make_async_remote_copy(
@@ -316,7 +321,13 @@
         src = (me + d) % n
         reduce_copy(1, send1, red1, src, src).wait_recv()
         sum1 = sum1 + red1[src]
-    masked = sum0 * mask_ref[mine, :]
+    seq = ids_ref.shape[1]
+    per = seq // part
+    ids = jnp.broadcast_to(ids_ref[pl.ds(me // per, 1), :], (part, seq))
+    row = lax.broadcasted_iota(jnp.int32, (part, seq), 0) + (me % per) * part
+    at = row == lax.broadcasted_iota(jnp.int32, (part, seq), 1)
+    mask = jnp.sum(jnp.where(at & (ids != 0), 1.0, 0.0), axis=1, keepdims=True)
+    masked = sum0 * mask
     sk[me, 0:64, :] = dot_tn(masked[:, 0:64], sum1)
     sk[me, 64:128, :] = dot_tn(masked[:, 128:192], sum0[:, 0:128])
 
@@ -358,12 +369,12 @@
     out_ref[...] = sk[...]
 
 
-def fused(x_act, gate_pre, up_pre, out_grad, down_weight, pi, pg, pu, ph, po, mask):
+def fused(x_act, gate_pre, up_pre, out_grad, down_weight, pi, pg, pu, ph, po, ids):
     rows, feat = x_act.shape
     ff = gate_pre.shape[1]
     half = feat // 2
     n = 8
-    rank = pi.shape[1]
+    rank = pi.shape[0]
     part = rows // n
     dma = pltpu.SemaphoreType.DMA
     vm = pltpu.VMEM
@@ -381,11 +392,11 @@
             vm((2, ff, half), BF16),
             vm((2, rows, TILE), BF16),
             vm((2, rows, TILE), BF16),
-            vm((feat, rank), BF16),
-            vm((ff, rank), BF16),
-            vm((ff, rank), BF16),
-            vm((ff, rank), BF16),
-            vm((feat, rank), BF16),
+            vm((rank, feat), BF16),
+            vm((rank, ff), BF16),
+            vm((rank, ff), BF16),
+            vm((rank, ff), BF16),
+            vm((rank, feat), BF16),
             vm((rows, rank), F32),
             vm((rows, rank), F32),
             vm((rows, rank), F32),
@@ -403,7 +414,7 @@
         cost_estimate=pl.CostEstimate(
             flops=2 * rows * ff * feat * n, bytes_accessed=2 * ff * feat * n, transcendentals=rows * ff
         ),
-    )(x_act, gate_pre, up_pre, out_grad, down_weight, pi, pg, pu, ph, po, mask)
+    )(x_act, gate_pre, up_pre, out_grad, down_weight, pi, pg, pu, ph, po, ids)
 
 
 VLIM = 66 * 1000 * 1000
@@ -428,13 +439,11 @@
     x_act, gate_pre, up_pre, out_grad, down_weight, proj_input, proj_gate, proj_up, proj_hidden,
     proj_output, target_sketch, token_ids, source_label,
 ):
-    rows = x_act.shape[0]
     cands = token_ids.shape[0]
     r = proj_input.shape[1]
-    mask = (token_ids != 0).astype(F32).reshape(rows, 1)
     parts = fused(
         x_act, gate_pre, up_pre, out_grad, down_weight,
-        proj_input, proj_gate, proj_up, proj_hidden, proj_output, mask,
+        proj_input.T, proj_gate.T, proj_up.T, proj_hidden.T, proj_output.T, token_ids,
     )
     mats = parts.reshape(cands, 8 // cands, 2 * r, 2 * r).sum(axis=1)
     sketch = jnp.concatenate(

time: 209 us -> 182 us (0.87)
  Pallas kernels: 189 us -> 175 us
  local copies, waits for them, and re-layouts: 11.9 us -> 0.5 us
    pallas_call x1, Pallas kernels: 189 us -> 175 us  [fused(): pl.pallas_call(fused_kernel, out_shape=jax.ShapeDtypeStruct((n, 2 * rank,...]
    unnamed x13 -> x8, local copies, waits for them, and re-layouts: 10.4 us -> 0.04 us
where the time goes in v2:
time: 182 us; the launch traced here: 181 us
  Pallas kernels  175 us (96%)
  blocking collectives  2.46 us (1%)
  other arithmetic  2.08 us (1%)
    pallas_call x1, Pallas kernels, fused(): pl.pallas_call(fused_kernel, out_shape=jax.ShapeDtypeStruct((n, 2 * rank,...  175 us

profile of v2, /device:TPU:0, one launch (start us, length us, event | category | flops | bytes accessed | tf_op | source)
XLA Modules:
  0.0 181.3 jit_solution(3570585041113024383)
XLA Ops:
  0.6 0.0 copy-start
  0.7 0.0 copy-start.2
  0.7 174.5 %shard_map.140 = f32[8,128,128]{2,1,0:T(8,128)} custom-call(bf16[768,1024]{1,0:T(8,128)(2,1)} %x_hbm.1, bf16[768,3584]{1,0:T(8,128)(2,1)} %g_hbm.1, bf16[768,3584]{1,0:T(8,128)(2,1)} %u_hbm.1, bf16[768,1024]{1,0:T(8,128)(2,1)} %og_hbm.1, bf16[3584,8192]{1,0:T(8,128)(2,1)} %w_hbm.1, bf16[64,1024]{1,0:T(8,128)(2,1)} %bitcast.12, bf16[64,3584]{1,0:T(8,128)(2,1)} %bitcast.9, ...), custom_call_target="tpu_custom_call" | custom-call | flops 45097156608 | bytes 58720256 | tf_op jit(solution)/shard_map/pallas_call | solution.py:382
  175.2 1.1 bitcast_reduce_fusion
  176.3 0.1 fusion.4
  176.4 0.1 reshape.27
  176.5 0.1 reshape.28
  176.7 0.1 reshape.29
  176.8 0.2 multiply_reduce_fusion
  177.0 0.0 copy-done
  177.0 0.8 convolution_multiply_fusion
  177.8 0.0 copy-done.2
  177.8 0.0 copy-start.1
  177.8 0.3 fusion.2
  178.1 0.1 convert_reduce_fusion
  178.2 2.5 %all-reduce = (f32[4,32]{1,0:T(4,128)S(1)}, f32[4]{0:T(128)S(1)}) all-reduce(f32[4,32]{1,0:T(4,128)S(1)} %fusion.2, f32[4]{0:T(128)S(1)} %convert_reduce_fusion), channel_id=1, replica_groups=mesh['groups'=2,'tensor'=8,'dp'=2] {'dp'}, use_global_device_ids=true, to_apply=%region_2.0 | all-reduce | flops 132 | bytes 1056 | tf_op jit(solution)/shard_map/psum | solution.py:433
  180.6 0.7 broadcast_divide_fusion
  181.3 0.0 copy-done.1
  (5 shorter events, 0.0 us)
Async XLA Ops:
  0.6 176.4 %copy-start = (bf16[32,12288]{1,0:T(8,128)(2,1)S(1)}, bf16[32,12288]{1,0:T(8,128)(2,1)}, u32[]{:S(2)}) copy-start(bf16[32,12288]{1,0:T(8,128)(2,1)} %param.23) | copy-start | bytes 2359300
  0.7 177.2 %copy-start.2 = (s32[4]{0:T(128)S(1)}, s32[4]{0:T(128)}, u32[]{:S(2)}) copy-start(s32[4]{0:T(128)} %param.25) | copy-start | bytes 52
  177.8 3.5 %copy-start.1 = (f32[4,32]{1,0:T(4,128)}, f32[4,32]{1,0:T(4,128)S(1)}, u32[]{:S(2)}) copy-start(f32[4,32]{1,0:T(4,128)S(1)} %convolution_multiply_fusion) | copy-start | bytes 1540
